TPU v7x, 128 devices: a whole 4x4x4 slice. The times are simulated.
128 devices in a mesh: expert: 32 (over z, x, core), dp: 4 (over y).
Axes of the slice: x: 4, y: 4, z: 4, core: 2. Of those that a mesh axis runs over, the one named last changes fastest.
Arguments:
- tokens: bfloat16 [24576, 1024], P(('expert', 'dp')), may hold values from -96 to 96
- out_grad: bfloat16 [24576, 1024], P(('expert', 'dp')), may hold values from -6 to 6
- routes: int32 [24576, 2], P(('expert', 'dp')), may hold values from 0 to 31, all different within a row
- router_weight: float32 [1024, 32], replicated, may hold values from -0.5 to 0.5
- gate_weight: bfloat16 [32, 2816, 1024], P('expert'), may hold values from -0.1875 to 0.1875
- up_weight: bfloat16 [32, 2816, 1024], P('expert'), may hold values from -0.1875 to 0.1875
- down_weight: bfloat16 [32, 2816, 1024], P('expert'), may hold values from -0.109375 to 0.109375
Outputs:
- in_grad: bfloat16 [24576, 1024], P(('expert', 'dp'))
- grad_experts: bfloat16 [32, 2816, 3, 1024], P('expert', 'dp')
- grad_router: float32 [1024, 32], replicated
Inputs may be any that keep to these rules, and one draw needn't show every extreme that they name: `routes`: each row names two different experts, and every expert is named by some row.
All inputs are finite; a program needn't handle non-finite values.
Results may differ from a plain program's by a relative error of at most 0.015.
Values may be sent and summed in bfloat16 or wider, within the bound.
No kernel may reach another device: no remote copies, remote signals or barrier semaphores. Data moves between devices by JAX's collectives and lax.ppermute only.
A program may use at most 192 MiB of HBM per device.

v0:
```python
import jax
import jax.numpy as jnp
from jax import lax
from jax.sharding import PartitionSpec as P

SQRT_TWO_OVER_PI = 0.7978845608
CUBIC_COEF = 0.044715


def gelu_parts(values):
    tanh_value = jnp.tanh(SQRT_TWO_OVER_PI * (values + CUBIC_COEF * values * values * values))
    gelu_value = 0.5 * values * (1.0 + tanh_value)
    gelu_slope = 0.5 * (1.0 + tanh_value) + 0.5 * values * (
        1.0 - tanh_value * tanh_value
    ) * SQRT_TWO_OVER_PI * (1.0 + 3.0 * CUBIC_COEF * values * values)
    return (gelu_value, gelu_slope)


def route_masks(routes, experts, capacity):
    count_tok = routes.shape[0]
    expert_ids = jnp.arange(experts, dtype=jnp.int32)
    onehot = (routes.T[:, :, None] == expert_ids[None, None, :]).astype(jnp.int32)
    flat_hits = onehot.reshape(2 * count_tok, experts)
    position = (
        jnp.sum(jnp.cumsum(flat_hits, 0, dtype=jnp.int32) * flat_hits, 1, dtype=jnp.int32) - 1
    )
    slot_index = routes.T.reshape(-1) * capacity + position
    slot_index = jnp.where(position < capacity, slot_index, -1).reshape(2, count_tok)
    slot_ids = jnp.arange(experts * capacity, dtype=jnp.int32)
    slot_masks = (slot_ids[None, :, None] == slot_index[:, None, :]).astype(jnp.bfloat16)
    return (onehot.astype(jnp.float32), slot_masks)


def source_side(tokens, out_grad, routes, router_weight, capacity):
    logits = jnp.dot(tokens.astype(jnp.float32), router_weight, precision=lax.Precision.HIGHEST)
    router_probs = jax.nn.softmax(logits, -1)
    onehot, slot_masks = route_masks(routes, router_weight.shape[1], capacity)
    gate_values = jnp.sum(onehot * router_probs[None], -1)
    scaled = (gate_values[:, :, None] * out_grad.astype(jnp.float32)[None]).astype(jnp.bfloat16)
    either_mask = slot_masks[0] + slot_masks[1]
    sent_rows = jnp.dot(either_mask, tokens, preferred_element_type=jnp.float32).astype(
        jnp.bfloat16
    )
    sent_grads = (
        jnp.dot(slot_masks[0], scaled[0], preferred_element_type=jnp.float32)
        + jnp.dot(slot_masks[1], scaled[1], preferred_element_type=jnp.float32)
    ).astype(jnp.bfloat16)
    return (router_probs, onehot, slot_masks, sent_rows, sent_grads)


def contract_rows(left, right):
    return lax.dot_general(
        left, right, (((0,), (0,)), ((), ())), preferred_element_type=jnp.float32
    )


def expert_pass(rows_x, rows_dy, w_gate, w_up, w_down):
    feature_dims = (((1,), (1,)), ((), ()))
    gate_pre = lax.dot_general(rows_x, w_gate, feature_dims, preferred_element_type=jnp.float32)
    up_pre = lax.dot_general(rows_x, w_up, feature_dims, preferred_element_type=jnp.float32)
    gelu_value, gelu_slope = gelu_parts(gate_pre)
    activated = (gelu_value * up_pre).astype(jnp.bfloat16)
    expert_outs = jnp.dot(activated, w_down, preferred_element_type=jnp.float32)
    hidden_grad = lax.dot_general(rows_dy, w_down, feature_dims, preferred_element_type=jnp.float32)
    pre_gate_grad = (hidden_grad * up_pre * gelu_slope).astype(jnp.bfloat16)
    pre_up_grad = (hidden_grad * gelu_value).astype(jnp.bfloat16)
    row_grads = jnp.dot(pre_gate_grad, w_gate, preferred_element_type=jnp.float32) + jnp.dot(
        pre_up_grad, w_up, preferred_element_type=jnp.float32
    )
    return (row_grads, expert_outs, activated, pre_gate_grad, pre_up_grad)


def weight_terms(rows_x, rows_dy, activated, pre_gate_grad, pre_up_grad):
    return jnp.stack(
        [
            contract_rows(pre_gate_grad, rows_x),
            contract_rows(pre_up_grad, rows_x),
            contract_rows(activated, rows_dy),
        ],
        1,
    )


def source_finish(
    tokens, out_grad, router_weight, router_probs, onehot, slot_masks, back_rows, back_outs
):
    either_mask = slot_masks[0] + slot_masks[1]
    expert_part = contract_rows(either_mask, back_rows)
    first_outs = contract_rows(slot_masks[0], back_outs)
    second_outs = contract_rows(slot_masks[1], back_outs)
    grad_float = out_grad.astype(jnp.float32)
    gate_grads = jnp.stack(
        [jnp.sum(grad_float * first_outs, -1), jnp.sum(grad_float * second_outs, -1)]
    )
    prob_grads = jnp.sum(onehot * gate_grads[:, :, None], 0)
    logit_grads = router_probs * (
        prob_grads - jnp.sum(router_probs * prob_grads, -1, keepdims=True)
    )
    in_grad = (
        expert_part + jnp.dot(logit_grads, router_weight.T, precision=lax.Precision.HIGHEST)
    ).astype(jnp.bfloat16)
    router_term = jnp.dot(
        tokens.astype(jnp.float32).T, logit_grads, precision=lax.Precision.HIGHEST
    )
    return (in_grad, router_term)


def shards(tokens, out_grad, routes, router_weight, gate_weight, up_weight, down_weight):
    count_tok = tokens.shape[0]
    features = tokens.shape[1]
    experts = router_weight.shape[1]
    capacity = 5 * count_tok * 2 // (4 * experts)
    router_probs, onehot, slot_masks, sent_rows, sent_grads = source_side(
        tokens, out_grad, routes, router_weight, capacity
    )
    rows_x, rows_dy = (
        lax.all_to_all(
            sent_rows.reshape(experts, capacity, features),
            "expert",
            split_axis=0,
            concat_axis=0,
            tiled=True,
        ),
        lax.all_to_all(
            sent_grads.reshape(experts, capacity, features),
            "expert",
            split_axis=0,
            concat_axis=0,
            tiled=True,
        ),
    )
    rows_x = rows_x.reshape(experts * capacity, features)
    rows_dy = rows_dy.reshape(experts * capacity, features)
    w_gate = gate_weight[0]
    w_up = up_weight[0]
    w_down = down_weight[0]
    row_grads, expert_outs, activated, pre_gate_grad, pre_up_grad = expert_pass(
        rows_x, rows_dy, w_gate, w_up, w_down
    )
    grads = lax.psum_scatter(
        weight_terms(rows_x, rows_dy, activated, pre_gate_grad, pre_up_grad).astype(jnp.bfloat16),
        "dp",
        scatter_dimension=0,
        tiled=True,
    )
    back_rows, back_outs = (
        lax.all_to_all(
            row_grads.astype(jnp.bfloat16).reshape(experts, capacity, features),
            "expert",
            split_axis=0,
            concat_axis=0,
            tiled=True,
        ),
        lax.all_to_all(
            expert_outs.astype(jnp.bfloat16).reshape(experts, capacity, features),
            "expert",
            split_axis=0,
            concat_axis=0,
            tiled=True,
        ),
    )
    in_grad, router_term = source_finish(
        tokens,
        out_grad,
        router_weight,
        router_probs,
        onehot,
        slot_masks,
        back_rows.reshape(experts * capacity, features),
        back_outs.reshape(experts * capacity, features),
    )
    grad_router = lax.psum(router_term, ("expert", "dp"))
    return (in_grad, grads[None], grad_router)


def solution(mesh):
    in_specs = (
        P(("expert", "dp"), None),
        P(("expert", "dp"), None),
        P(("expert", "dp"), None),
        P(),
        P("expert", None, None),
        P("expert", None, None),
        P("expert", None, None),
    )
    out_specs = (P(("expert", "dp"), None), P("expert", "dp", None, None), P())
    return jax.shard_map(shards, mesh=mesh, in_specs=in_specs, out_specs=out_specs, check_vma=False)
```

profile of v0, /device:TPU:1, one launch (start us, length us, event | category | flops | bytes accessed | tf_op | source)
XLA Modules:
  0.0 320.7 jit_solution(5410827507848277592)
XLA Ops:
  8.0 0.0 copy-start
  8.0 0.8 eq.46
  8.8 0.8 eq.50
  9.6 0.9 reduce-window.6
  10.5 0.2 slice_reduce_fusion
  10.7 0.1 fusion.30
  10.8 0.1 sub.26
  10.9 0.7 compare_select_fusion
  11.6 0.2 iota_compare_fusion
  11.9 0.0 copy-done
  11.9 0.4 convolution_convert_fusion
  12.3 0.3 reshape.72
  12.6 26.4 %all_to_all.20 = bf16[32,15,1024]{2,1,0:T(8,128)(2,1)S(1)} all-to-all(bf16[32,15,1024]{2,1,0:T(8,128)(2,1)S(1)} %reshape.72), channel_id=1, replica_groups=mesh['expert'=32,'dp'=4] {'expert'}, dimensions={0} | all-to-all | bytes 1966080 | tf_op jit(solution)/shard_map/all_to_all | solution.py:117
  39.0 0.3 reshape.73
  39.3 0.0 copy-start.2
  39.3 0.0 slice-start
  39.4 6.0 %fusion.2 = f32[480,2816]{1,0:T(8,128)S(1)} fusion(bf16[480,1024]{1,0:T(8,128)(2,1)S(1)} %reshape.73, bf16[1,2816,1024]{2,1,0:T(8,128)(2,1)} %param.11), kind=kOutput, calls=%fused_computation.5 | convolution fusion | flops 2768240640 | bytes 12156928 | tf_op jit(solution)/shard_map/dot_general | solution.py:59
  45.4 0.0 copy-done.2
  45.4 0.0 copy-start.6
  45.4 0.0 slice-start.1
  45.4 10.6 %multiply_convert_fusion = (bf16[480,2816]{1,0:T(8,128)(2,1)S(1)}, f32[480,2816]{1,0:T(8,128)}) fusion(f32[480,2816]{1,0:T(8,128)S(1)} %fusion.2, bf16[480,1024]{1,0:T(8,128)(2,1)S(1)} %reshape.73, bf16[1,2816,1024]{2,1,0:T(8,128)(2,1)} %param.12), kind=kOutput, calls=%fused_computation.25 | convolution fusion | flops 2781757440 | bytes 20267008 | tf_op jit(solution)/shard_map/dot_general | solution.py:60
  56.0 0.0 copy-done.6
  56.0 1.5 copy-done.7
  57.5 0.0 slice-done
  57.6 0.0 slice-done.1
  57.6 3.0 fusion.21
  60.5 1.3 reshape.76
  61.8 4.1 %all-to-all-start.3 = ((bf16[32,15,1024]{2,1,0:T(8,128)(2,1)}), bf16[32,15,1024]{2,1,0:T(8,128)(2,1)S(1)}, u32[]{:S(2)}, u32[]{:S(2)}) async-start(bf16[32,15,1024]{2,1,0:T(8,128)(2,1)} %reshape.76), calls=%async_computation.3 | async-start | bytes 2097152 | tf_op jit(solution)/shard_map/all_to_all | solution.py:154
  65.9 1.1 convert_element_type.52
  67.0 0.0 copy-done.4
  67.0 0.5 fusion.38
  67.5 15.7 %all-to-all-done.3 = bf16[32,15,1024]{2,1,0:T(8,128)(2,1)S(1)} async-done(((bf16[32,15,1024]{2,1,0:T(8,128)(2,1)}), bf16[32,15,1024]{2,1,0:T(8,128)(2,1)S(1)}, u32[]{:S(2)}, u32[]{:S(2)}) %all-to-all-start.3) | async-done | bytes 983072 | tf_op jit(solution)/shard_map/all_to_all | solution.py:154
  83.2 1.3 reshape.77
  84.5 1.8 fusion.26
  86.3 1.8 fusion.25
  88.2 0.1 multiply_convert_fusion.2
  88.4 0.4 fusion.27
  88.8 0.4 add_convert_fusion.1
  89.2 1.3 reshape.70
  90.5 4.0 %all-to-all-start = ((bf16[32,15,1024]{2,1,0:T(8,128)(2,1)}), bf16[32,15,1024]{2,1,0:T(8,128)(2,1)S(1)}, u32[]{:S(2)}, u32[]{:S(2)}) async-start(bf16[32,15,1024]{2,1,0:T(8,128)(2,1)} %reshape.70), calls=%async_computation | async-start | bytes 2097152 | tf_op jit(solution)/shard_map/all_to_all | solution.py:124
  94.5 0.0 all-reduce.2.cloned.1.call-start
  94.6 0.9 convolution_bitcast_fusion
  95.5 0.0 all-reduce.2.cloned.1.call-update
  95.5 0.0 reduce-scatter.2.cloned.1.call-start
  95.6 16.2 %all-to-all-done = bf16[32,15,1024]{2,1,0:T(8,128)(2,1)S(1)} async-done(((bf16[32,15,1024]{2,1,0:T(8,128)(2,1)}), bf16[32,15,1024]{2,1,0:T(8,128)(2,1)S(1)}, u32[]{:S(2)}, u32[]{:S(2)}) %all-to-all-start) | async-done | bytes 983072 | tf_op jit(solution)/shard_map/all_to_all | solution.py:124
  111.8 0.3 reshape.71
  112.1 5.2 %convert_bitcast_fusion = bf16[2816,1,1024]{2,0,1:T(8,128)(2,1)S(1)} fusion(bf16[480,2816]{1,0:T(8,128)(2,1)} %copy-done.7, bf16[480,1024]{1,0:T(8,128)(2,1)S(1)} %reshape.71), kind=kOutput, calls=%fused_computation.15 | convolution fusion | flops 2771124224 | bytes 9453568 | tf_op jit(solution)/shard_map/dot_general | solution.py:52
  117.3 12.3 %multiply_convert_fusion.1 = (bf16[480,2816]{1,0:T(8,128)(2,1)S(1)}, bf16[480,2816]{1,0:T(8,128)(2,1)S(1)}) fusion(f32[480,2816]{1,0:T(8,128)} %copy-done.6, f32[480,2816]{1,0:T(8,128)} %get-tuple-element.10, bf16[480,1024]{1,0:T(8,128)(2,1)S(1)} %reshape.71, bf16[1,2816,1024]{2,1,0:T(8,128)(2,1)} %param.13), kind=kOutput, calls=%fused_computation.26 | convolution fusion | flops 2799329280 | bytes 22970368 | tf_op jit(solution)/shard_map/dot_general | solution.py:64
  129.7 3.5 %convert_bitcast_fusion.1 = bf16[2816,1,1024]{2,0,1:T(8,128)(2,1)S(1)} fusion(bf16[480,2816]{1,0:T(8,128)(2,1)S(1)} %get-tuple-element.5, bf16[480,1024]{1,0:T(8,128)(2,1)S(1)} %copy-done.3), kind=kOutput, calls=%fused_computation.16 | convolution fusion | flops 2771124224 | bytes 9453568 | tf_op jit(solution)/shard_map/dot_general | solution.py:52
  133.1 3.5 %convert_bitcast_fusion.2 = bf16[2816,1,1024]{2,0,1:T(8,128)(2,1)S(1)} fusion(bf16[480,2816]{1,0:T(8,128)(2,1)S(1)} %get-tuple-element.6, bf16[480,1024]{1,0:T(8,128)(2,1)S(1)} %copy-done.3), kind=kOutput, calls=%fused_computation.17 | convolution fusion | flops 2771124224 | bytes 9453568 | tf_op jit(solution)/shard_map/dot_general | solution.py:52
  136.6 7.2 %pad_maximum_fusion = bf16[2816,3,1024]{2,0,1:T(8,128)(2,1)} fusion(bf16[2816,1,1024]{2,0,1:T(8,128)(2,1)S(1)} %convert_bitcast_fusion, bf16[2816,1,1024]{2,0,1:T(8,128)(2,1)S(1)} %convert_bitcast_fusion.1, bf16[2816,1,1024]{2,0,1:T(8,128)(2,1)S(1)} %convert_bitcast_fusion.2), kind=kLoop, calls=%fused_computation | loop fusion | flops 17301504 | bytes 34603008 | tf_op jit(solution)/shard_map/stack | solution.py:74
  143.8 0.0 reduce-scatter.2.cloned.1.call-update
  143.8 5.9 %fusion = f32[480,1024]{1,0:T(8,128)S(1)} fusion(bf16[480,2816]{1,0:T(8,128)(2,1)} %copy-done.10, bf16[1,2816,1024]{2,1,0:T(8,128)(2,1)} %param.11), kind=kOutput, calls=%fused_computation.3 | convolution fusion | flops 2768240640 | bytes 10436608 | tf_op jit(solution)/shard_map/dot_general | solution.py:67
  149.8 0.0 copy-done.9
  149.8 0.0 copy-start.1
  149.8 6.3 %add_convert_fusion = bf16[480,1024]{1,0:T(8,128)(2,1)S(1)} fusion(f32[480,1024]{1,0:T(8,128)S(1)} %fusion, bf16[480,2816]{1,0:T(8,128)(2,1)S(1)} %copy-done.9, bf16[1,2816,1024]{2,1,0:T(8,128)(2,1)} %param.12), kind=kOutput, calls=%fused_computation.28 | convolution fusion | flops 2769223680 | bytes 11419648 | tf_op jit(solution)/shard_map/dot_general | solution.py:67
  156.1 0.3 reshape.74
  156.4 20.4 %all_to_all.21 = bf16[32,15,1024]{2,1,0:T(8,128)(2,1)S(1)} all-to-all(bf16[32,15,1024]{2,1,0:T(8,128)(2,1)S(1)} %reshape.74), channel_id=1, replica_groups=mesh['expert'=32,'dp'=4] {'expert'}, dimensions={0} | all-to-all | bytes 1966080 | tf_op jit(solution)/shard_map/all_to_all | solution.py:147
  176.8 0.3 reshape.75
  177.1 0.4 fusion.32
  177.5 1.6 fusion.24
  179.1 132.5 %all-reduce.2.cloned.1.call-done = f32[1024,32]{0,1:T(8,128)} async-done(((f32[1024,32]{0,1:T(8,128)}), f32[1024,32]{0,1:T(8,128)}) %all-reduce.2.cloned.1.call-update) | async-done | bytes 131088 | tf_op jit(solution)/shard_map/psum | solution.py:172
  311.6 1.6 copy.18
  313.2 0.0 copy-done.1
  (21 shorter events, 0.2 us)
Async XLA Ops:
  8.0 3.9 %copy-start = (bf16[192,1024]{1,0:T(8,128)(2,1)S(1)}, bf16[192,1024]{1,0:T(8,128)(2,1)}, u32[]{:S(2)}) copy-start(bf16[192,1024]{1,0:T(8,128)(2,1)} %param.7) | copy-start | bytes 1179652
  39.3 6.1 %copy-start.2 = (bf16[480,1024]{1,0:T(8,128)(2,1)}, bf16[480,1024]{1,0:T(8,128)(2,1)S(1)}, u32[]{:S(2)}) copy-start(bf16[480,1024]{1,0:T(8,128)(2,1)S(1)} %reshape.73) | copy-start | bytes 2949124
  39.3 18.2 %slice-start = ((s8[5767168]{0:T(1024)(128)(4,1)}), s8[4194304]{0:T(1024)(128)(4,1)S(1)}, s32[]{:S(2)}) async-start(s8[5767168]{0:T(1024)(128)(4,1)} %bitcast.96), calls=%async_computation.7 | async-start | bytes 8388608
  45.4 10.6 %copy-start.6 = (f32[480,2816]{1,0:T(8,128)}, f32[480,2816]{1,0:T(8,128)S(1)}, u32[]{:S(2)}) copy-start(f32[480,2816]{1,0:T(8,128)S(1)} %fusion.2) | copy-start | bytes 16220164
  45.4 12.2 %slice-start.1 = ((s8[5767168]{0:T(1024)(128)(4,1)}), s8[1572864]{0:T(1024)(128)(4,1)S(1)}, s32[]{:S(2)}) async-start(s8[5767168]{0:T(1024)(128)(4,1)} %bitcast.96), calls=%async_computation.8 | async-start | bytes 3145728
  56.0 1.5 copy-start.7
  57.6 9.4 %copy-start.4 = (f32[1024,32]{0,1:T(8,128)S(1)}, f32[1024,32]{0,1:T(8,128)}, u32[]{:S(2)}) copy-start(f32[1024,32]{0,1:T(8,128)} %param.10) | copy-start | bytes 393220
  61.8 26.4 %copy-start.5 = (s32[192,2]{0,1:T(2,128)S(1)}, s32[192,2]{0,1:T(2,128)}, u32[]{:S(2)}) copy-start(s32[192,2]{0,1:T(2,128)} %param.9) | copy-start | bytes 4612
  61.8 21.4 %all-to-all-start.3 = ((bf16[32,15,1024]{2,1,0:T(8,128)(2,1)}), bf16[32,15,1024]{2,1,0:T(8,128)(2,1)S(1)}, u32[]{:S(2)}, u32[]{:S(2)}) async-start(bf16[32,15,1024]{2,1,0:T(8,128)(2,1)} %reshape.76), calls=%async_computation.3 | async-start | bytes 2097152 | tf_op jit(solution)/shard_map/all_to_all | solution.py:154
  90.5 21.3 %all-to-all-start = ((bf16[32,15,1024]{2,1,0:T(8,128)(2,1)}), bf16[32,15,1024]{2,1,0:T(8,128)(2,1)S(1)}, u32[]{:S(2)}, u32[]{:S(2)}) async-start(bf16[32,15,1024]{2,1,0:T(8,128)(2,1)} %reshape.70), calls=%async_computation | async-start | bytes 2097152 | tf_op jit(solution)/shard_map/all_to_all | solution.py:124
  94.5 217.2 %all-reduce.2.cloned.1.call-start = ((), (), s32[]{:S(2)}) async-start(), calls=%async_computation.6 | async-start | bytes 262144 | tf_op jit(solution)/shard_map/psum | solution.py:172
  95.5 216.1 %reduce-scatter.2.cloned.1.call-start = ((), (), s32[]{:S(2)}) async-start(), calls=%async_computation.5 | async-start | bytes 21626880 | tf_op jit(solution)/shard_map/reduce_scatter | solution.py:140
  117.3 12.4 %copy-start.3 = (bf16[480,1024]{1,0:T(8,128)(2,1)S(1)}, bf16[480,1024]{1,0:T(8,128)(2,1)}, u32[]{:S(2)}) copy-start(bf16[480,1024]{1,0:T(8,128)(2,1)} %copy-done.2) | copy-start | bytes 2949124
  129.6 3.5 %copy-start.8 = (bf16[480,2816]{1,0:T(8,128)(2,1)}, bf16[480,2816]{1,0:T(8,128)(2,1)S(1)}, u32[]{:S(2)}) copy-start(bf16[480,2816]{1,0:T(8,128)(2,1)S(1)} %get-tuple-element.5) | copy-start | bytes 8110084
  129.6 3.5 %copy-start.10 = (bf16[480,2816]{1,0:T(8,128)(2,1)}, bf16[480,2816]{1,0:T(8,128)(2,1)S(1)}, u32[]{:S(2)}) copy-start(bf16[480,2816]{1,0:T(8,128)(2,1)S(1)} %get-tuple-element.6) | copy-start | bytes 8110084
  143.8 6.0 %copy-start.9 = (bf16[480,2816]{1,0:T(8,128)(2,1)S(1)}, bf16[480,2816]{1,0:T(8,128)(2,1)}, u32[]{:S(2)}) copy-start(bf16[480,2816]{1,0:T(8,128)(2,1)} %copy-done.8) | copy-start | bytes 8110084
  149.8 163.4 %copy-start.1 = (bf16[192,1024]{1,0:T(8,128)(2,1)S(1)}, bf16[192,1024]{1,0:T(8,128)(2,1)}, u32[]{:S(2)}) copy-start(bf16[192,1024]{1,0:T(8,128)(2,1)} %param.7) | copy-start | bytes 1179652
Sparse Core Ops, SparseCore 0:
  100.6 210.9 all-reduce.1
Sparse Core Ops, SparseCore 1:
  143.9 149.9 reduce-scatter.1
where the time goes:
time: 321 us
  waiting for transfers between devices  164 us (51%)
  matrix products  64.6 us (20%)
  blocking collectives  46.8 us (15%)
  between operations  15.8 us (5%)
  other arithmetic  10.5 us (3%)
  local copies, waits for them, and re-layouts  10.4 us (3%)
  starting transfers between devices  8.18 us (3%)
    psum x1, waiting for transfers between devices, shards(): grad_router = lax.psum(router_term, ('expert', 'dp'))  133 us
    all_to_all x1, blocking collectives, shards(): lax.all_to_all(sent_rows.reshape(experts, capacity, features), 'expert',...  26.4 us
    all_to_all x1, blocking collectives, shards(): lax.all_to_all(row_grads.astype(jnp.bfloat16).reshape(experts, capacity,...  20.4 us
    dot_general x6, matrix products, contract_rows(): lax.dot_general(left, right, (((0,), (0,)), ((), ())), preferred_element_...  16.2 us
    all_to_all x1, waiting for transfers between devices, shards(): lax.all_to_all(sent_grads.reshape(experts, capacity, features), 'expert',...  16.2 us
    all_to_all x1, waiting for transfers between devices, shards(): lax.all_to_all(expert_outs.astype(jnp.bfloat16).reshape(experts, capacity...  15.7 us
    dot_general x1, matrix products, expert_pass(): lax.dot_general(rows_dy, w_down, feature_dims, preferred_element_type=jnp...  12.3 us
    dot_general x1, matrix products, expert_pass(): lax.dot_general(rows_x, w_up, feature_dims, preferred_element_type=jnp.fl...  10.6 us
  transfers between devices with their start and end apart: 4, of which 3 were waited for; matrix products, arithmetic and copies ran while one was open for 15% of the time, Pallas kernels for 0%

commit v1 on v0

v1 whole, which is shorter than its diff:
```python
import functools
import jax
import jax.numpy as jnp
from jax import lax
from jax.experimental import pallas as pl
from jax.experimental.pallas import tpu as pltpu
from jax.sharding import PartitionSpec as P

SQRT_TWO_OVER_PI = 0.7978845608
CUBIC_COEF = 0.044715
STRIDE = 16
F32 = jnp.float32
BF16 = jnp.bfloat16
VMEM_LIMIT = 60 * 1024 * 1024

FEATURE_DIMS = (((1,), (1,)), ((), ()))
ROW_DIMS = (((0,), (0,)), ((), ()))


def dot(left, right, dims=(((1,), (0,)), ((), ()))):
    return lax.dot_general(left, right, dims, preferred_element_type=F32)


def gelu_parts(values):
    square = values * values
    tanh_value = jnp.tanh(values * (SQRT_TWO_OVER_PI + (SQRT_TWO_OVER_PI * CUBIC_COEF) * square))
    half = 0.5 + 0.5 * tanh_value
    slope = half + (half * (1.0 - tanh_value)) * values * (
        SQRT_TWO_OVER_PI + (3.0 * CUBIC_COEF * SQRT_TWO_OVER_PI) * square
    )
    return (values * half, slope)


def split_three(values):
    high = values.astype(BF16)
    rest = values - high.astype(F32)
    mid = rest.astype(BF16)
    low = (rest - mid.astype(F32)).astype(BF16)
    return (high, mid, low)


def softmax(logits, axis):
    shifted = jnp.exp(logits - jnp.max(logits, axis, keepdims=True))
    return shifted / jnp.sum(shifted, axis, keepdims=True)


def slot_rows(routes, experts, capacity):
    count_tok = routes.shape[1]
    expert_ids = lax.broadcasted_iota(jnp.int32, (experts, count_tok), 0)
    first = expert_ids == routes[0:1, :]
    second = expert_ids == routes[1:2, :]
    earlier = (
        lax.broadcasted_iota(jnp.int32, (count_tok, count_tok), 0)
        < lax.broadcasted_iota(jnp.int32, (count_tok, count_tok), 1)
    ).astype(BF16)
    first_hits = first.astype(F32)
    second_hits = second.astype(F32)
    first_before = dot(first_hits.astype(BF16), earlier)
    second_before = dot(second_hits.astype(BF16), earlier) + jnp.sum(first_hits, 1, keepdims=True)
    first_pos = jnp.sum(first_hits * first_before, 0, keepdims=True)
    second_pos = jnp.sum(second_hits * second_before, 0, keepdims=True)
    slots = []
    for pos, route in ((first_pos, routes[0:1, :]), (second_pos, routes[1:2, :])):
        pos = pos.astype(jnp.int32)
        slots.append(jnp.where(pos < capacity, route * STRIDE + pos, -1))
    return slots


def slot_mask(slots, experts):
    count_tok = slots[0].shape[1]
    slot_ids = lax.broadcasted_iota(jnp.int32, (experts * STRIDE, count_tok), 0)
    return ((slot_ids == slots[0]) | (slot_ids == slots[1])).astype(F32).astype(BF16)


def dispatch_kernel(experts, capacity, tokens, out_grad, routes, sent_rows, sent_grads):
    mask = slot_mask(slot_rows(routes[...], experts, capacity), experts)
    sent_rows[...] = dot(mask, tokens[...]).astype(BF16)
    sent_grads[...] = dot(mask, out_grad[...]).astype(BF16)


def combine_kernel(experts, capacity, routes, back, in_grad):
    mask = slot_mask(slot_rows(routes[...], experts, capacity), experts)
    in_grad[...] = dot(mask, back[...], ROW_DIMS).astype(BF16)


def expert_kernel(
    expert, rows_x, rows_g, router, w_gate, w_up, w_down, row_grads, router_term, total, gates, hits
):
    step = pl.program_id(0)
    last = pl.num_programs(0) - 1

    @pl.when(step == 0)
    def _():
        high, mid, low = split_three(router[...])
        stacked = jnp.concatenate([high, mid, low], 0)
        count = router.shape[0]
        parts = dot(rows_x[...], stacked, FEATURE_DIMS)
        logits = parts[:, :count] + parts[:, count : 2 * count] + parts[:, 2 * count :]
        gates[...] = softmax(logits, 1)
        total[...] = jnp.zeros_like(total)
        hits[...] = jnp.zeros_like(hits)

    probs = gates[...]
    mine = lax.broadcasted_iota(jnp.int32, probs.shape, 1) == expert[0]
    gate = jnp.sum(jnp.where(mine, probs, 0.0), 1, keepdims=True)
    gate_pre = dot(rows_x[...], w_gate[...], FEATURE_DIMS)
    up_pre = dot(rows_x[...], w_up[...], FEATURE_DIMS)
    raw_grad = dot(rows_g[...], w_down[...], FEATURE_DIMS)
    gelu_value, gelu_slope = gelu_parts(gate_pre)
    hits[...] += jnp.sum(gelu_value * up_pre * raw_grad, 1, keepdims=True)
    hidden_grad = raw_grad * gate
    pre_gate_grad = (hidden_grad * up_pre * gelu_slope).astype(BF16)
    pre_up_grad = (hidden_grad * gelu_value).astype(BF16)
    total[...] += dot(pre_gate_grad, w_gate[...]) + dot(pre_up_grad, w_up[...])

    @pl.when(step == last)
    def _():
        high, mid, low = split_three(router[...])
        logit_grads = hits[...] * gate * (mine.astype(F32) - probs)
        logit_high = logit_grads.astype(BF16)
        logit_low = (logit_grads - logit_high.astype(F32)).astype(BF16)
        router_part = dot(logit_high, high) + dot(logit_high, mid) + dot(logit_low, high)
        row_grads[...] = (total[...] + router_part).astype(BF16)
        router_term[...] = dot(logit_high, rows_x[...], ROW_DIMS) + dot(
            logit_low, rows_x[...], ROW_DIMS
        )


def weight_kernel(pieces, first, last, *refs):
    place, router, w_gate, w_up, w_down = refs[:5]
    rows = refs[5 : 5 + 2 * pieces]
    rest = refs[5 + 2 * pieces :]
    if first:
        (out,) = rest
    else:
        before, out = rest
    high, mid, low = split_three(router[...])
    stacked = jnp.concatenate([high, mid, low], 0)
    count = router.shape[0]
    sums = [None, None, None] if first else [before[k] for k in range(3)]
    for piece in range(pieces):
        rows_x = rows[2 * piece][...]
        rows_g = rows[2 * piece + 1][...]
        parts = dot(stacked, rows_x, FEATURE_DIMS)
        probs = softmax(parts[:count] + parts[count : 2 * count] + parts[2 * count :], 0)
        mine = lax.broadcasted_iota(jnp.int32, probs.shape, 0) == place[0]
        gate = jnp.sum(jnp.where(mine, probs, 0.0), 0, keepdims=True)
        gate_pre = dot(w_gate[...], rows_x, FEATURE_DIMS)
        up_pre = dot(w_up[...], rows_x, FEATURE_DIMS)
        hidden_grad = dot(w_down[...], rows_g, FEATURE_DIMS) * gate
        gelu_value, gelu_slope = gelu_parts(gate_pre)
        activated = (gelu_value * up_pre * gate).astype(BF16)
        pre_gate_grad = (hidden_grad * up_pre * gelu_slope).astype(BF16)
        pre_up_grad = (hidden_grad * gelu_value).astype(BF16)
        terms = (dot(pre_gate_grad, rows_x), dot(pre_up_grad, rows_x), dot(activated, rows_g))
        sums = [t if s is None else s + t for s, t in zip(sums, terms)]
    for k in range(3):
        out[k] = sums[k].astype(out.dtype)


def run_dispatch(tokens, out_grad, routes, experts, capacity):
    shape = jax.ShapeDtypeStruct((experts * STRIDE, tokens.shape[1]), BF16)
    return pl.pallas_call(
        functools.partial(dispatch_kernel, experts, capacity),
        out_shape=(shape, shape),
        compiler_params=pltpu.CompilerParams(vmem_limit_bytes=VMEM_LIMIT),
        name="dispatch",
    )(tokens, out_grad, routes)


def run_combine(routes, back, experts, capacity):
    return pl.pallas_call(
        functools.partial(combine_kernel, experts, capacity),
        out_shape=jax.ShapeDtypeStruct((routes.shape[1], back.shape[1]), BF16),
        compiler_params=pltpu.CompilerParams(vmem_limit_bytes=VMEM_LIMIT),
        name="combine",
    )(routes, back)


def run_expert(expert, rows_x, rows_g, router, w_gate, w_up, w_down, tile=256):
    rows, features = rows_x.shape
    hidden = w_gate.shape[1]
    experts = router.shape[0]
    whole = lambda shape: pl.BlockSpec(shape, lambda i: (0, 0))
    weight = pl.BlockSpec((None, tile, features), lambda i: (0, i, 0))
    return pl.pallas_call(
        expert_kernel,
        grid=(hidden // tile,),
        in_specs=[
            pl.BlockSpec(memory_space=pltpu.SMEM),
            whole((rows, features)),
            whole((rows, features)),
            whole((experts, features)),
            weight,
            weight,
            weight,
        ],
        out_specs=(whole((rows, features)), whole((experts, features))),
        out_shape=(
            jax.ShapeDtypeStruct((rows, features), BF16),
            jax.ShapeDtypeStruct((experts, features), F32),
        ),
        scratch_shapes=[
            pltpu.VMEM((rows, features), F32),
            pltpu.VMEM((rows, experts), F32),
            pltpu.VMEM((rows, 1), F32),
        ],
        compiler_params=pltpu.CompilerParams(vmem_limit_bytes=VMEM_LIMIT),
        cost_estimate=pl.CostEstimate(
            flops=10 * rows * hidden * features,
            bytes_accessed=6 * hidden * features + 6 * rows * features,
            transcendentals=rows * hidden,
        ),
        name="expert_pass",
    )(expert, rows_x, rows_g, router, w_gate, w_up, w_down)


def run_weight(place, router, weights, pieces, before, out_dtype, slices, tile):
    features = router.shape[1]
    hidden = weights[0].shape[1] // slices
    steps = hidden // tile
    whole = lambda shape: pl.BlockSpec(shape, lambda i, p: (0, 0))
    weight = pl.BlockSpec((None, tile, features), lambda i, p: (0, p[1] * steps + i, 0))
    grads = pl.BlockSpec((3, tile, features), lambda i, p: (0, i, 0))
    rows = [r for piece in pieces for r in piece]
    count = sum(x.shape[0] for x, _ in pieces)
    return pl.pallas_call(
        functools.partial(weight_kernel, len(pieces), before is None, True),
        grid_spec=pltpu.PrefetchScalarGridSpec(
            num_scalar_prefetch=1,
            grid=(steps,),
            in_specs=[whole(router.shape), weight, weight, weight]
            + [whole(r.shape) for r in rows]
            + ([] if before is None else [grads]),
            out_specs=grads,
        ),
        out_shape=jax.ShapeDtypeStruct((3, hidden, features), out_dtype),
        compiler_params=pltpu.CompilerParams(vmem_limit_bytes=VMEM_LIMIT),
        cost_estimate=pl.CostEstimate(
            flops=12 * count * hidden * features,
            bytes_accessed=6 * hidden * features + 4 * count * features + 12 * hidden * features,
            transcendentals=count * hidden,
        ),
        name="weight_grads",
    )(place, router, *weights, *rows, *([] if before is None else [before]))


def exchange(rows, axis, stride):
    return lax.all_to_all(rows, axis, split_axis=0, concat_axis=0, tiled=True)


def shift(value, axis, step):
    size = lax.axis_size(axis)
    return lax.ppermute(value, axis, [(i, (i + step) % size) for i in range(size)])


def sum_over(value, axis):
    size = lax.axis_size(axis)
    bit = 1
    while bit < size:
        value = value + lax.ppermute(value, axis, [(i, i ^ bit) for i in range(size)])
        bit *= 2
    return value


def shards(tokens, out_grad, routes, router_weight, gate_weight, up_weight, down_weight):
    count_tok, features = tokens.shape
    experts = router_weight.shape[1]
    capacity = 5 * count_tok * 2 // (4 * experts)
    routes_t = routes.T
    router = router_weight.T
    weights = (gate_weight, up_weight, down_weight)
    expert = lax.axis_index("expert").astype(jnp.int32)
    group = lax.axis_index("dp").astype(jnp.int32)

    sent_rows, sent_grads = run_dispatch(tokens, out_grad, routes_t, experts, capacity)

    def arrive(sent):
        got = lax.all_to_all(
            sent.reshape(experts, STRIDE, features),
            "expert",
            split_axis=0,
            concat_axis=0,
            tiled=True,
        )
        return got[:, :capacity].reshape(experts * capacity, features)

    rows_x = arrive(sent_rows)
    rows_g = arrive(sent_grads)
    half = rows_x.shape[0] // 2
    left_x, right_x = shift(rows_x, "dp", 1), shift(rows_x, "dp", -1)
    left_g, right_g = shift(rows_g, "dp", 1), shift(rows_g, "dp", -1)
    far_x = (shift(left_x[:half], "dp", 1), shift(right_x[half:], "dp", -1))
    far_g = (shift(left_g[:half], "dp", 1), shift(right_g[half:], "dp", -1))

    row_grads, router_term = run_expert(
        jnp.stack([expert]), rows_x, rows_g, router, *weights
    )
    back = jnp.pad(
        row_grads.reshape(experts, capacity, features), ((0, 0), (0, STRIDE - capacity), (0, 0))
    )
    back = lax.all_to_all(back, "expert", split_axis=0, concat_axis=0, tiled=True)
    in_grad = run_combine(routes_t, back.reshape(-1, features), experts, capacity)
    grad_router = sum_over(sum_over(router_term, "expert"), "dp").T

    place = jnp.stack([expert, group])
    slices = lax.axis_size("dp")
    near = run_weight(
        place,
        router,
        weights,
        [(rows_x, rows_g), (left_x, left_g), (right_x, right_g)],
        None,
        F32,
        slices,
        352,
    )
    grads = run_weight(
        place,
        router,
        weights,
        list(zip(far_x, far_g)),
        near,
        BF16,
        slices,
        352,
    )
    return (in_grad, jnp.transpose(grads, (1, 0, 2))[None], grad_router)


def solution(mesh):
    in_specs = (
        P(("expert", "dp"), None),
        P(("expert", "dp"), None),
        P(("expert", "dp"), None),
        P(),
        P("expert", None, None),
        P("expert", None, None),
        P("expert", None, None),
    )
    out_specs = (P(("expert", "dp"), None), P("expert", "dp", None, None), P())
    return jax.shard_map(shards, mesh=mesh, in_specs=in_specs, out_specs=out_specs, check_vma=False)
```

time: 321 us -> 200 us (0.62)
  waiting for transfers between devices: 164 us -> 56.3 us
  Pallas kernels: 0 us -> 74.1 us
  matrix products: 64.6 us -> 0 us
  blocking collectives: 46.8 us -> 26.6 us
  starting transfers between devices: 8.18 us -> 26.9 us
  between operations: 15.8 us -> 0.76 us
  other arithmetic: 10.5 us -> 2.23 us
    psum x1 -> x0, waiting for transfers between devices: 133 us -> none  [shards(): grad_router = lax.psum(router_term, ('expert', 'dp'))]
    pallas_call x0 -> x5, Pallas kernels: none -> 74.1 us  [the longest x2 35 us: run_weight(): pl.pallas_call(functools.partial(weight_kernel, len(pieces), before is No...]
    dot_general x18 -> x0, matrix products: 64.6 us -> none  [the longest x6 16.2 us: contract_rows(): lax.dot_general(left, right, (((0,), (0,)), ((), ())), preferred_element_...]
    ppermute x0 -> x15, waiting for transfers between devices: none -> 40.3 us  [the longest x7 40.3 us: sum_over(): lax.ppermute(value, axis, [(i, i ^ bit) for i in range(size)])]
    all_to_all x2 -> x1, blocking collectives: 46.8 us -> 26.6 us  [arrive(): lax.all_to_all(sent.reshape(experts, STRIDE, features), 'expert', split_a...]
    ppermute x0 -> x15, starting transfers between devices: none -> 16.5 us  [the longest x8 8.81 us: shift(): lax.ppermute(value, axis, [(i, (i + step) % size) for i in range(size)])]
    all_to_all x2, waiting for transfers between devices: 31.8 us -> 16 us  [the longest x1 16 us: arrive(): lax.all_to_all(sent.reshape(experts, STRIDE, features), 'expert', split_a...]
    another operation x4 -> x1, other arithmetic: 8.11 us -> 0.55 us  [shards(): place = jnp.stack([expert, group])]
  transfers between devices with their start and end apart: 4 -> 17, of which waited for: 3 -> 7; matrix products, arithmetic and copies ran while one was open for 15% -> 5% of each run, Pallas kernels for 0% -> 13%
where the time goes in v1:
time: 200 us; the launch traced here: 199 us
  Pallas kernels  74.1 us (37%)
  waiting for transfers between devices  56.3 us (28%)
  starting transfers between devices  26.9 us (13%)
  blocking collectives  26.6 us (13%)
  local copies, waits for them, and re-layouts  12 us (6%)
  other arithmetic  2.23 us (1%)
    ppermute x7, waiting for transfers between devices, sum_over(): lax.ppermute(value, axis, [(i, i ^ bit) for i in range(size)])  40.3 us
    pallas_call x2, Pallas kernels, run_weight(): pl.pallas_call(functools.partial(weight_kernel, len(pieces), before is No...  35 us
    pallas_call x1, Pallas kernels, run_expert(): pl.pallas_call(expert_kernel, grid=(hidden // tile,), in_specs=[pl.BlockS...  33.5 us
    all_to_all x1, blocking collectives, arrive(): lax.all_to_all(sent.reshape(experts, STRIDE, features), 'expert', split_a...  26.6 us
    all_to_all x1, waiting for transfers between devices, arrive(): lax.all_to_all(sent.reshape(experts, STRIDE, features), 'expert', split_a...  16 us
    ppermute x8, starting transfers between devices, shift(): lax.ppermute(value, axis, [(i, (i + step) % size) for i in range(size)])  8.81 us
    ppermute x7, starting transfers between devices, sum_over(): lax.ppermute(value, axis, [(i, i ^ bit) for i in range(size)])  7.66 us
    all_to_all x1, starting transfers between devices, shards(): lax.all_to_all(back, 'expert', split_axis=0, concat_axis=0, tiled=True)  6.47 us
  transfers between devices with their start and end apart: 17, of which 7 were waited for; matrix products, arithmetic and copies ran while one was open for 5% of the time, Pallas kernels for 13%

profile of v1, /device:TPU:1, one launch (start us, length us, event | category | flops | bytes accessed | tf_op | source)
XLA Modules:
  0.0 199.0 jit_solution(13206154194757756892)
XLA Ops:
  0.6 3.0 %dispatch.1 = (bf16[512,1024]{1,0:T(8,128)(2,1)}, bf16[512,1024]{1,0:T(8,128)(2,1)}) custom-call(bf16[192,1024]{1,0:T(8,128)(2,1)} %tokens.1, bf16[192,1024]{1,0:T(8,128)(2,1)} %out_grad.1, s32[2,192]{1,0:T(2,128)} %bitcast.23), custom_call_target="tpu_custom_call" | custom-call | tf_op jit(solution)/shard_map/dispatch/pallas_call | solution.py:163
  3.7 26.6 %all_to_all.15 = bf16[32,16,1024]{2,1,0:T(8,128)(2,1)S(1)} all-to-all(bf16[32,16,1024]{2,1,0:T(8,128)(2,1)} %bitcast.19), channel_id=1, replica_groups=mesh['expert'=32,'dp'=4] {'expert'}, dimensions={0} | all-to-all | bytes 2097152 | tf_op jit(solution)/shard_map/all_to_all | solution.py:279
  30.3 4.0 %all-to-all-start.1 = ((bf16[32,16,1024]{2,1,0:T(8,128)(2,1)}), bf16[32,16,1024]{2,1,0:T(8,128)(2,1)S(1)}, u32[]{:S(2)}, u32[]{:S(2)}) async-start(bf16[32,16,1024]{2,1,0:T(8,128)(2,1)} %bitcast.18), calls=%async_computation.1 | async-start | bytes 2097152 | tf_op jit(solution)/shard_map/all_to_all | solution.py:279
  34.3 1.3 reshape.25.rows_x.refs_5_
  35.6 16.0 %all-to-all-done.1 = bf16[32,16,1024]{2,1,0:T(8,128)(2,1)S(1)} async-done(((bf16[32,16,1024]{2,1,0:T(8,128)(2,1)}), bf16[32,16,1024]{2,1,0:T(8,128)(2,1)S(1)}, u32[]{:S(2)}, u32[]{:S(2)}) %all-to-all-start.1) | async-done | bytes 1048608 | tf_op jit(solution)/shard_map/all_to_all | solution.py:279
  51.5 1.3 reshape.27.rows_g.refs_6_
  52.8 0.0 copy-start.1
  52.8 0.0 copy-start.2
  52.8 33.5 %expert_pass.1 = (bf16[480,1024]{1,0:T(8,128)(2,1)}, f32[32,1024]{1,0:T(8,128)}) custom-call(s32[1]{0:T(128)} %bitcast.1.expert, bf16[480,1024]{1,0:T(8,128)(2,1)} %reshape.25.rows_x.refs_5_, bf16[480,1024]{1,0:T(8,128)(2,1)} %reshape.27.rows_g.refs_6_, f32[32,1024]{1,0:T(8,128)} %bitcast.20, bf16[1,2816,1024]{2,1,0:T(8,128)(2,1)} %refs_2_.3, ...), custom_call_target="tpu_custom_call" | custom-call | flops 13841203200 | bytes 20250624 | tf_op jit(solution)/shard_map/expert_pass/pallas_call | solution.py:186
  86.4 0.4 collective-permute-start.8
  86.8 1.2 collective-permute-done.8
  88.0 0.9 add.23
  88.9 0.4 collective-permute-start.9
  89.3 0.0 copy-done.1
  89.3 1.3 collective-permute-start
  90.6 0.0 copy-done.2
  90.6 1.3 collective-permute-start.2
  91.9 1.4 collective-permute-start.4
  93.3 0.3 collective-permute-start.6
  93.6 0.1 collective-permute-done.9
  93.7 2.1 %collective-permute-start.10 = (f32[32,1024]{1,0:T(8,128)S(1)}, f32[32,1024]{1,0:T(8,128)S(1)}, u32[]{:S(2)}, u32[]{:S(2)}) collective-permute-start(f32[32,1024]{1,0:T(8,128)S(1)} %add.24), channel_id=1, source_target_pairs={{0,16},{4,20},{8,24},{12,28},{16,0},{20,4},{24,8},{28,12},{32,48},... | collective-permute-start | bytes 393224 | tf_op jit(solution)/shard_map/ppermute | solution.py:261
  95.8 3.3 %collective-permute-done.10 = f32[32,1024]{1,0:T(8,128)S(1)} collective-permute-done((f32[32,1024]{1,0:T(8,128)S(1)}, f32[32,1024]{1,0:T(8,128)S(1)}, u32[]{:S(2)}, u32[]{:S(2)}) %collective-permute-start.10) | collective-permute-done | bytes 131104 | tf_op jit(solution)/shard_map/ppermute | solution.py:261
  99.1 0.4 collective-permute-start.11
  99.5 3.9 %collective-permute-done.11 = f32[32,1024]{1,0:T(8,128)S(1)} collective-permute-done((f32[32,1024]{1,0:T(8,128)S(1)}, f32[32,1024]{1,0:T(8,128)S(1)}, u32[]{:S(2)}, u32[]{:S(2)}) %collective-permute-start.11) | collective-permute-done | bytes 131104 | tf_op jit(solution)/shard_map/ppermute | solution.py:261
  103.5 1.3 collective-permute-start.12
  104.7 4.1 %collective-permute-done.12 = f32[32,1024]{1,0:T(8,128)S(1)} collective-permute-done((f32[32,1024]{1,0:T(8,128)S(1)}, f32[32,1024]{1,0:T(8,128)S(1)}, u32[]{:S(2)}, u32[]{:S(2)}) %collective-permute-start.12) | collective-permute-done | bytes 131104 | tf_op jit(solution)/shard_map/ppermute | solution.py:261
  108.9 1.5 collective-permute-start.13
  110.4 27.6 %collective-permute-done.13 = f32[32,1024]{1,0:T(8,128)S(1)} collective-permute-done((f32[32,1024]{1,0:T(8,128)S(1)}, f32[32,1024]{1,0:T(8,128)S(1)}, u32[]{:S(2)}, u32[]{:S(2)}) %collective-permute-start.13) | collective-permute-done | bytes 131104 | tf_op jit(solution)/shard_map/ppermute | solution.py:261
  138.0 1.6 collective-permute-start.14
  139.6 0.6 pad_add_fusion.refs_0_
  140.2 1.5 reshape.28
  141.7 1.1 pad.4
  142.8 6.5 %all-to-all-start.2 = ((bf16[32,16,1024]{2,1,0:T(8,128)(2,1)}), bf16[32,16,1024]{2,1,0:T(8,128)(2,1)S(1)}, u32[]{:S(2)}, u32[]{:S(2)}) async-start(bf16[32,16,1024]{2,1,0:T(8,128)(2,1)} %pad.4), calls=%async_computation.2 | async-start | bytes 2097152 | tf_op jit(solution)/shard_map/all_to_all | solution.py:302
  149.3 0.0 collective-permute-done.14
  149.3 0.7 add_bitcast_fusion
  150.0 0.0 collective-permute-done.refs_7_
  150.0 1.1 slice.26
  151.0 0.1 collective-permute-start.1
  151.1 0.0 collective-permute-done.2.refs_8_
  151.1 1.9 slice.27
  153.0 1.2 collective-permute-start.3
  154.2 0.0 collective-permute-done.4.refs_9_
  154.2 1.1 slice.28
  155.3 1.5 collective-permute-start.5
  156.8 0.0 collective-permute-done.6.refs_10_
  156.8 1.1 slice.29
  157.9 1.7 collective-permute-start.7
  159.6 22.7 %weight_grads.2.refs_9_ = f32[3,704,1024]{2,1,0:T(8,128)} custom-call(s32[2]{0:T(128)} %pad_add_fusion.refs_0_, f32[32,1024]{1,0:T(8,128)} %bitcast.21, bf16[1,2816,1024]{2,1,0:T(8,128)(2,1)} %refs_2_.3, bf16[1,2816,1024]{2,1,0:T(8,128)(2,1)} %refs_3_.3, bf16[1,2816,1024]{2,1,0:T(8,128)(2,1)} %refs_4_.3, bf16[480,1024]{1,0:T(8,128)(2,1)} %reshape.25.rows_x.refs_5_, ...), custom_call_target="tpu_custom_call" | custom-call | flops 12457082880 | bytes 18874368 | tf_op jit(solution)/shard_map/weight_grads/pallas_call | solution.py:227
  182.3 0.0 all-to-all-done.2
  182.3 0.0 copy-start
  182.3 1.0 copy-done
  183.3 2.6 %combine.1 = bf16[192,1024]{1,0:T(8,128)(2,1)} custom-call(s32[2,192]{1,0:T(2,128)} %bitcast.24, bf16[512,1024]{1,0:T(8,128)(2,1)} %bitcast.15), custom_call_target="tpu_custom_call" | custom-call | tf_op jit(solution)/shard_map/combine/pallas_call | solution.py:172
  185.8 0.0 collective-permute-done.1.refs_5_
  185.8 0.0 collective-permute-done.3.refs_6_
  185.8 0.0 collective-permute-done.5.refs_7_
  185.8 0.0 collective-permute-done.7.refs_8_
  185.8 0.0 copy-start.3
  185.9 0.8 copy-done.3
  186.7 12.3 %weight_grads.3 = bf16[3,704,1024]{2,1,0:T(8,128)(2,1)} custom-call(s32[2]{0:T(128)} %pad_add_fusion.refs_0_, f32[32,1024]{1,0:T(8,128)} %bitcast.22, bf16[1,2816,1024]{2,1,0:T(8,128)(2,1)} %refs_2_.3, bf16[1,2816,1024]{2,1,0:T(8,128)(2,1)} %refs_3_.3, bf16[1,2816,1024]{2,1,0:T(8,128)(2,1)} %refs_4_.3, bf16[240,1024]{1,0:T(8,128)(2,1)} %collective-permute-done.1.refs_5_, ...), custom_call_target="tpu_custom_call" | custom-call | flops 4152360960 | bytes 14942208 | tf_op jit(solution)/shard_map/weight_grads/pallas_call | solution.py:227
  (5 shorter events, 0.1 us)
Async XLA Ops:
  30.3 21.3 %all-to-all-start.1 = ((bf16[32,16,1024]{2,1,0:T(8,128)(2,1)}), bf16[32,16,1024]{2,1,0:T(8,128)(2,1)S(1)}, u32[]{:S(2)}, u32[]{:S(2)}) async-start(bf16[32,16,1024]{2,1,0:T(8,128)(2,1)} %bitcast.18), calls=%async_computation.1 | async-start | bytes 2097152 | tf_op jit(solution)/shard_map/all_to_all | solution.py:279
  52.8 36.5 %copy-start.1 = (bf16[480,1024]{1,0:T(8,128)(2,1)S(1)}, bf16[480,1024]{1,0:T(8,128)(2,1)}, u32[]{:S(2)}) copy-start(bf16[480,1024]{1,0:T(8,128)(2,1)} %reshape.25.rows_x.refs_5_) | copy-start | bytes 2949124
  52.8 37.8 %copy-start.2 = (bf16[480,1024]{1,0:T(8,128)(2,1)S(1)}, bf16[480,1024]{1,0:T(8,128)(2,1)}, u32[]{:S(2)}) copy-start(bf16[480,1024]{1,0:T(8,128)(2,1)} %reshape.27.rows_g.refs_6_) | copy-start | bytes 2949124
  86.4 1.6 collective-permute-start.8
  88.9 4.8 %collective-permute-start.9 = (f32[32,1024]{1,0:T(8,128)S(1)}, f32[32,1024]{1,0:T(8,128)S(1)}, u32[]{:S(2)}, u32[]{:S(2)}) collective-permute-start(f32[32,1024]{1,0:T(8,128)S(1)} %add.23), channel_id=1, source_target_pairs={{0,8},{4,12},{8,0},{12,4},{16,24},{20,28},{24,16},{28,20},{32,40},... | collective-permute-start | bytes 393224 | tf_op jit(solution)/shard_map/ppermute | solution.py:261
  89.3 60.7 %collective-permute-start = (bf16[480,1024]{1,0:T(8,128)(2,1)S(1)}, bf16[480,1024]{1,0:T(8,128)(2,1)}, u32[]{:S(2)}, u32[]{:S(2)}) collective-permute-start(bf16[480,1024]{1,0:T(8,128)(2,1)S(1)} %copy-done.1), channel_id=1, source_target_pairs={{0,1},{1,2},{2,3},{3,0},{4,5},{5,6},{6,7},{7,4},{8,9},{9,10},{10,1... | collective-permute-start | bytes 2949128 | tf_op jit(solution)/shard_map/ppermute | solution.py:254
  90.6 60.5 %collective-permute-start.2 = (bf16[480,1024]{1,0:T(8,128)(2,1)S(1)}, bf16[480,1024]{1,0:T(8,128)(2,1)}, u32[]{:S(2)}, u32[]{:S(2)}) collective-permute-start(bf16[480,1024]{1,0:T(8,128)(2,1)S(1)} %copy-done.2), channel_id=1, source_target_pairs={{0,1},{1,2},{2,3},{3,0},{4,5},{5,6},{6,7},{7,4},{8,9},{9,10},{10,1... | collective-permute-start | bytes 2949128 | tf_op jit(solution)/shard_map/ppermute | solution.py:254
  91.9 62.3 %collective-permute-start.4 = (bf16[480,1024]{1,0:T(8,128)(2,1)S(1)}, bf16[480,1024]{1,0:T(8,128)(2,1)}, u32[]{:S(2)}, u32[]{:S(2)}) collective-permute-start(bf16[480,1024]{1,0:T(8,128)(2,1)S(1)} %copy-done.1), channel_id=1, source_target_pairs={{0,3},{1,0},{2,1},{3,2},{4,7},{5,4},{6,5},{7,6},{8,11},{9,8},{10,9... | collective-permute-start | bytes 2949128 | tf_op jit(solution)/shard_map/ppermute | solution.py:254
  93.3 63.5 %collective-permute-start.6 = (bf16[480,1024]{1,0:T(8,128)(2,1)S(1)}, bf16[480,1024]{1,0:T(8,128)(2,1)}, u32[]{:S(2)}, u32[]{:S(2)}) collective-permute-start(bf16[480,1024]{1,0:T(8,128)(2,1)S(1)} %copy-done.2), channel_id=1, source_target_pairs={{0,3},{1,0},{2,1},{3,2},{4,7},{5,4},{6,5},{7,6},{8,11},{9,8},{10,9... | collective-permute-start | bytes 2949128 | tf_op jit(solution)/shard_map/ppermute | solution.py:254
  93.7 5.4 %collective-permute-start.10 = (f32[32,1024]{1,0:T(8,128)S(1)}, f32[32,1024]{1,0:T(8,128)S(1)}, u32[]{:S(2)}, u32[]{:S(2)}) collective-permute-start(f32[32,1024]{1,0:T(8,128)S(1)} %add.24), channel_id=1, source_target_pairs={{0,16},{4,20},{8,24},{12,28},{16,0},{20,4},{24,8},{28,12},{32,48},... | collective-permute-start | bytes 393224 | tf_op jit(solution)/shard_map/ppermute | solution.py:261
  99.1 4.3 %collective-permute-start.11 = (f32[32,1024]{1,0:T(8,128)S(1)}, f32[32,1024]{1,0:T(8,128)S(1)}, u32[]{:S(2)}, u32[]{:S(2)}) collective-permute-start(f32[32,1024]{1,0:T(8,128)S(1)} %add.25), channel_id=1, source_target_pairs={{0,32},{4,36},{8,40},{12,44},{16,48},{20,52},{24,56},{28,60},{32,0... | collective-permute-start | bytes 393224 | tf_op jit(solution)/shard_map/ppermute | solution.py:261
  103.5 5.4 %collective-permute-start.12 = (f32[32,1024]{1,0:T(8,128)S(1)}, f32[32,1024]{1,0:T(8,128)S(1)}, u32[]{:S(2)}, u32[]{:S(2)}) collective-permute-start(f32[32,1024]{1,0:T(8,128)S(1)} %add.26), channel_id=1, source_target_pairs={{0,64},{4,68},{8,72},{12,76},{16,80},{20,84},{24,88},{28,92},{32,9... | collective-permute-start | bytes 393224 | tf_op jit(solution)/shard_map/ppermute | solution.py:261
  108.9 29.1 %collective-permute-start.13 = (f32[32,1024]{1,0:T(8,128)S(1)}, f32[32,1024]{1,0:T(8,128)S(1)}, u32[]{:S(2)}, u32[]{:S(2)}) collective-permute-start(f32[32,1024]{1,0:T(8,128)S(1)} %add.27), channel_id=1, source_target_pairs={{0,1},{1,0},{2,3},{3,2},{4,5},{5,4},{6,7},{7,6},{8,9},{9,8},{10,11... | collective-permute-start | bytes 393224 | tf_op jit(solution)/shard_map/ppermute | solution.py:261
  138.0 11.3 %collective-permute-start.14 = (f32[32,1024]{1,0:T(8,128)S(1)}, f32[32,1024]{1,0:T(8,128)S(1)}, u32[]{:S(2)}, u32[]{:S(2)}) collective-permute-start(f32[32,1024]{1,0:T(8,128)S(1)} %add.28), channel_id=1, source_target_pairs={{0,2},{1,3},{2,0},{3,1},{4,6},{5,7},{6,4},{7,5},{8,10},{9,11},{10,... | collective-permute-start | bytes 393224 | tf_op jit(solution)/shard_map/ppermute | solution.py:261
  142.8 39.5 %all-to-all-start.2 = ((bf16[32,16,1024]{2,1,0:T(8,128)(2,1)}), bf16[32,16,1024]{2,1,0:T(8,128)(2,1)S(1)}, u32[]{:S(2)}, u32[]{:S(2)}) async-start(bf16[32,16,1024]{2,1,0:T(8,128)(2,1)} %pad.4), calls=%async_computation.2 | async-start | bytes 2097152 | tf_op jit(solution)/shard_map/all_to_all | solution.py:302
  151.0 34.8 %collective-permute-start.1 = (bf16[240,1024]{1,0:T(8,128)(2,1)S(1)}, bf16[240,1024]{1,0:T(8,128)(2,1)}, u32[]{:S(2)}, u32[]{:S(2)}) collective-permute-start(bf16[240,1024]{1,0:T(8,128)(2,1)S(1)} %slice.26), channel_id=1, source_target_pairs={{0,1},{1,2},{2,3},{3,0},{4,5},{5,6},{6,7},{7,4},{8,9},{9,10},{10,1... | collective-permute-start | bytes 1474568 | tf_op jit(solution)/shard_map/ppermute | solution.py:254
  153.0 32.8 %collective-permute-start.3 = (bf16[240,1024]{1,0:T(8,128)(2,1)}, bf16[240,1024]{1,0:T(8,128)(2,1)}, u32[]{:S(2)}, u32[]{:S(2)}) collective-permute-start(bf16[240,1024]{1,0:T(8,128)(2,1)} %slice.27), channel_id=1, source_target_pairs={{0,1},{1,2},{2,3},{3,0},{4,5},{5,6},{6,7},{7,4},{8,9},{9,10},{10,1... | collective-permute-start | bytes 1474568 | tf_op jit(solution)/shard_map/ppermute | solution.py:254
  155.3 30.5 %collective-permute-start.5 = (bf16[240,1024]{1,0:T(8,128)(2,1)S(1)}, bf16[240,1024]{1,0:T(8,128)(2,1)}, u32[]{:S(2)}, u32[]{:S(2)}) collective-permute-start(bf16[240,1024]{1,0:T(8,128)(2,1)S(1)} %slice.28), channel_id=1, source_target_pairs={{0,3},{1,0},{2,1},{3,2},{4,7},{5,4},{6,5},{7,6},{8,11},{9,8},{10,9... | collective-permute-start | bytes 1474568 | tf_op jit(solution)/shard_map/ppermute | solution.py:254
  157.9 28.0 %collective-permute-start.7 = (bf16[240,1024]{1,0:T(8,128)(2,1)S(1)}, bf16[240,1024]{1,0:T(8,128)(2,1)S(1)}, u32[]{:S(2)}, u32[]{:S(2)}) collective-permute-start(bf16[240,1024]{1,0:T(8,128)(2,1)S(1)} %slice.29), channel_id=1, source_target_pairs={{0,3},{1,0},{2,1},{3,2},{4,7},{5,4},{6,5},{7,6},{8,11},{9,8},{10,9... | collective-permute-start | bytes 1474568 | tf_op jit(solution)/shard_map/ppermute | solution.py:254
  182.3 1.0 copy-start
  185.8 0.8 copy-start.3
